TPU v7x, 32 devices: a whole 2x2x4 slice. The times are simulated.
32 devices in a mesh: replica: 8 (over z, core), shard: 4 (over y, x).
Axes of the slice: x: 2, y: 2, z: 4, core: 2. Of those that a mesh axis runs over, the one named last changes fastest.
Arguments:
- tokens: bfloat16 [32768, 640], P(('replica', 'shard')), may hold values from -6 to 6
- positions: int32 [32768], P(('replica', 'shard')), may hold values from 0 to 1023, as said below
- cotangent: bfloat16 [32768, 640], P(('replica', 'shard')), may hold values from -6 to 6
- q_weight: bfloat16 [640, 1024], P('shard'), may hold values from -0.25 to 0.25
- k_weight: bfloat16 [640, 256], P('shard'), may hold values from -0.25 to 0.25
- v_weight: bfloat16 [640, 256], P('shard'), may hold values from -0.25 to 0.25
- o_weight: bfloat16 [1024, 640], P('shard'), may hold values from -0.1875 to 0.1875
- gate_weight: bfloat16 [640, 2048], P('shard'), may hold values from -0.25 to 0.25
- up_weight: bfloat16 [640, 2048], P('shard'), may hold values from -0.25 to 0.25
- down_weight: bfloat16 [2048, 640], P('shard'), may hold values from -0.125 to 0.125
- attn_gain: bfloat16 [640], P('shard'), may hold values from 0.099609375 to 1.8984375
- query_gain: bfloat16 [256], P('shard'), may hold values from 0.099609375 to 1.8984375
- key_gain: bfloat16 [256], P('shard'), may hold values from 0.099609375 to 1.8984375
- post_attn_gain: bfloat16 [640], P('shard'), may hold values from 0.099609375 to 1.8984375
- pre_ffn_gain: bfloat16 [640], P('shard'), may hold values from 0.099609375 to 1.8984375
- post_ffn_gain: bfloat16 [640], P('shard'), may hold values from 0.099609375 to 1.8984375
Outputs:
- mixed: bfloat16 [32768, 640], P(('replica', 'shard'))
- tokens_grad: float32 [32768, 640], P(('replica', 'shard'))
- q_weight_grad: float32 [640, 1024], P('shard')
- k_weight_grad: float32 [640, 256], P('shard')
- v_weight_grad: float32 [640, 256], P('shard')
- o_weight_grad: float32 [1024, 640], P('shard')
- gate_weight_grad: float32 [640, 2048], P('shard')
- up_weight_grad: float32 [640, 2048], P('shard')
- down_weight_grad: float32 [2048, 640], P('shard')
- attn_gain_grad: float32 [640], P('shard')
- query_gain_grad: float32 [256], P('shard')
- key_gain_grad: float32 [256], P('shard')
- post_attn_gain_grad: float32 [640], P('shard')
- pre_ffn_gain_grad: float32 [640], P('shard')
- post_ffn_gain_grad: float32 [640], P('shard')
Inputs may be any that keep to these rules, and one draw needn't show every extreme that they name: `positions`: each aligned block of 1024 tokens holds one to three documents laid end to end; a token's position counts from the start of its document, which never lies before its block's start; in some block one document fills the whole block.
All inputs are finite; a program needn't handle non-finite values.
Results may differ from a plain program's by a relative error of at most 0.015.
Values may be sent and summed in bfloat16 or wider, within the bound.
A program may use at most 192 MiB of HBM per device.

v0:
```python
import math

import jax
import jax.numpy as jnp
from jax import lax
from jax.sharding import PartitionSpec as P

HEAD = 256
WINDOW = 512


EPSILON = 1e-06


def rms_scale(values, scale_gain):
    return (
        values * lax.rsqrt(jnp.mean(values * values, axis=-1, keepdims=True) + EPSILON) * scale_gain
    )


def rotary_angles(positions, head_width):
    indices = jnp.arange(head_width // 2).astype(jnp.float32)
    frequency = 10000.0 ** (-2.0 * indices / head_width)
    return positions.astype(jnp.float32)[:, None] * frequency[None, :]


def rotate(values, angles):
    half_width = values.shape[-1] // 2
    cosine = jnp.cos(angles)[:, None, :]
    sine_part = jnp.sin(angles)[:, None, :]
    front_half = values[..., :half_width]
    back_half = values[..., half_width:]
    return jnp.concatenate(
        [front_half * cosine - back_half * sine_part, back_half * cosine + front_half * sine_part],
        axis=-1,
    )


def prepare_heads(raw_rows, scale_gain, angles, factor):
    length = raw_rows.shape[0]
    shaped = raw_rows.reshape(length, -1, scale_gain.shape[0])
    return (rotate(rms_scale(shaped, scale_gain), angles) * factor).reshape(length, -1)


def visible_keys(start, query_pos, window):
    row_index = start + jnp.arange(window, dtype=jnp.int32)
    col_index = start - window + jnp.arange(2 * window, dtype=jnp.int32)
    distance = row_index[:, None] - col_index[None, :]
    return (distance >= 0) & (distance < window) & (distance <= query_pos[:, None])


def window_view(rows_in, blocks, window):
    padded = jnp.concatenate(
        [jnp.zeros((window, rows_in.shape[1]), rows_in.dtype), rows_in], axis=0
    )
    padded = padded.reshape(blocks + 1, window, rows_in.shape[1])
    return jnp.concatenate([padded[:-1], padded[1:]], axis=1)


def fold_windows(window_grads, blocks):
    window = window_grads.shape[1] // 2
    front_part = window_grads[:, :window]
    back_part = window_grads[:, window:]
    empty = jnp.zeros_like(front_part[:1])
    summed = jnp.concatenate([front_part, empty], axis=0) + jnp.concatenate(
        [empty, back_part], axis=0
    )
    return summed[1:].reshape(blocks * window, -1)


def block_scores(queries, key_rows, query_pos, start):
    window = queries.shape[0]
    shaped = queries.reshape(window, -1, key_rows.shape[1])
    scores = jnp.einsum("qhd,kd->hqk", shaped, key_rows, preferred_element_type=jnp.float32)
    return (jnp.where(visible_keys(start, query_pos, window)[None], scores, -1e30), shaped)


def attend_forward(block_item):
    queries, key_rows, value_rows, query_pos, start = block_item
    scores, shaped = block_scores(queries, key_rows, query_pos, start)
    highest = jnp.max(scores, axis=-1, keepdims=True)
    raised = jnp.exp(scores - highest)
    summed = jnp.sum(raised, axis=-1, keepdims=True)
    shares = (raised / summed).astype(jnp.bfloat16)
    result = jnp.einsum("hqk,kd->qhd", shares, value_rows, preferred_element_type=jnp.float32)
    return (result.reshape(queries.shape[0], -1), highest + jnp.log(summed))


def attend_backward(block_item):
    queries, key_rows, value_rows, query_pos, start, log_total, out_grad = block_item
    scores, shaped = block_scores(queries, key_rows, query_pos, start)
    shares = jnp.exp(scores - log_total)
    grad_shaped = out_grad.reshape(shaped.shape)
    share_grad = jnp.einsum(
        "qhd,kd->hqk", grad_shaped, value_rows, preferred_element_type=jnp.float32
    )
    scores_low = (
        shares * (share_grad - jnp.sum(shares * share_grad, axis=-1, keepdims=True))
    ).astype(jnp.bfloat16)
    query_grad = jnp.einsum("hqk,kd->qhd", scores_low, key_rows, preferred_element_type=jnp.float32)
    key_grad = jnp.einsum("hqk,qhd->kd", scores_low, shaped, preferred_element_type=jnp.float32)
    value_grad = jnp.einsum(
        "hqk,qhd->kd", shares.astype(jnp.bfloat16), grad_shaped, preferred_element_type=jnp.float32
    )
    return (query_grad.reshape(queries.shape[0], -1), key_grad, value_grad)


def gelu_product(gate, upward):
    return jax.nn.gelu(gate, approximate=True) * upward


def pack_owners(gradients, owners, replicas):
    flattened = jnp.concatenate([member.reshape(owners, -1) for member in gradients], axis=1)
    return flattened.reshape(owners, replicas, -1).transpose(1, 0, 2).reshape(owners * replicas, -1)


def unpack_owner(flattened, shapes):
    result = []
    offset = 0
    for member_shape in shapes:
        length = math.prod(member_shape)
        result.append(flattened[offset : offset + length].reshape(member_shape))
        offset += length
    return tuple(result)


def body(
    tokens,
    positions,
    cotangent,
    q_weight,
    k_weight,
    v_weight,
    o_weight,
    gate_weight,
    up_weight,
    down_weight,
    attn_gain,
    query_gain,
    key_gain,
    post_attn_gain,
    pre_ffn_gain,
    post_ffn_gain,
):
    owned = (
        q_weight,
        k_weight,
        v_weight,
        o_weight,
        gate_weight,
        up_weight,
        down_weight,
        attn_gain,
        query_gain,
        key_gain,
        post_attn_gain,
        pre_ffn_gain,
        post_ffn_gain,
    )
    gathered = (
        lax.all_gather(q_weight, "shard", axis=0, tiled=True),
        lax.all_gather(k_weight, "shard", axis=0, tiled=True),
        lax.all_gather(v_weight, "shard", axis=0, tiled=True),
        lax.all_gather(o_weight, "shard", axis=0, tiled=True),
        lax.all_gather(gate_weight, "shard", axis=0, tiled=True),
        lax.all_gather(up_weight, "shard", axis=0, tiled=True),
        lax.all_gather(down_weight, "shard", axis=0, tiled=True),
        lax.all_gather(attn_gain, "shard", axis=0, tiled=True),
        lax.all_gather(query_gain, "shard", axis=0, tiled=True),
        lax.all_gather(key_gain, "shard", axis=0, tiled=True),
        lax.all_gather(post_attn_gain, "shard", axis=0, tiled=True),
        lax.all_gather(pre_ffn_gain, "shard", axis=0, tiled=True),
        lax.all_gather(post_ffn_gain, "shard", axis=0, tiled=True),
    )
    q_full, k_full, v_full, o_full, gate_full, up_full, down_full = gathered[:7]
    gain_attn, gain_query, gain_key, gain_post_attn, gain_pre_ffn, gain_post_ffn = (
        member.astype(jnp.float32) for member in gathered[7:]
    )
    length = tokens.shape[0]
    window = WINDOW
    blocks = length // window
    inputs = tokens.astype(jnp.float32)
    angles = rotary_angles(positions, HEAD)
    starts = jnp.arange(blocks, dtype=jnp.int32) * window
    normed_f, pull_attn_norm = jax.vjp(rms_scale, inputs, gain_attn)
    normed = normed_f.astype(jnp.bfloat16)
    query_raw = jnp.dot(normed, q_full, preferred_element_type=jnp.float32)
    key_raw = jnp.dot(normed, k_full, preferred_element_type=jnp.float32)
    values = jnp.dot(normed, v_full, preferred_element_type=jnp.float32).astype(jnp.bfloat16)
    queries_f, pull_query = jax.vjp(
        lambda raw_rows, scale_gain: prepare_heads(raw_rows, scale_gain, angles, HEAD ** (-0.5)),
        query_raw,
        gain_query,
    )
    key_f, pull_key = jax.vjp(
        lambda raw_rows, scale_gain: prepare_heads(raw_rows, scale_gain, angles, 1.0),
        key_raw,
        gain_key,
    )
    queries = queries_f.astype(jnp.bfloat16)
    key_rows = key_f.astype(jnp.bfloat16)
    query_blocks = queries.reshape(blocks, window, -1)
    key_windows = window_view(key_rows, blocks, window)
    value_windows = window_view(values, blocks, window)
    place_blocks = positions.reshape(blocks, window)
    attended_f, log_totals = lax.map(
        attend_forward, (query_blocks, key_windows, value_windows, place_blocks, starts)
    )
    attended = attended_f.reshape(length, -1).astype(jnp.bfloat16)
    branch = jnp.dot(attended, o_full, preferred_element_type=jnp.float32)
    post_attn_f, pull_post_attn = jax.vjp(rms_scale, branch, gain_post_attn)
    middle = inputs + post_attn_f
    inner_f, pull_pre_ffn = jax.vjp(rms_scale, middle, gain_pre_ffn)
    inner = inner_f.astype(jnp.bfloat16)
    gate = jnp.dot(inner, gate_full, preferred_element_type=jnp.float32)
    upward = jnp.dot(inner, up_full, preferred_element_type=jnp.float32)
    hidden_f, pull_glu = jax.vjp(gelu_product, gate, upward)
    hidden = hidden_f.astype(jnp.bfloat16)
    ffn_out = jnp.dot(hidden, down_full, preferred_element_type=jnp.float32)
    post_ffn_f, pull_post_ffn = jax.vjp(rms_scale, ffn_out, gain_post_ffn)
    mixed = (middle + post_ffn_f).astype(jnp.bfloat16)
    upstream = cotangent.astype(jnp.float32)
    ffn_grad, post_ffn_gain_grad = pull_post_ffn(upstream)
    ffn_low = ffn_grad.astype(jnp.bfloat16)
    down_grad = jnp.einsum("sf,sd->fd", hidden, ffn_low, preferred_element_type=jnp.float32)
    hidden_grad = jnp.einsum("sd,fd->sf", ffn_low, down_full, preferred_element_type=jnp.float32)
    gate_grad, up_grad = pull_glu(hidden_grad)
    gate_low = gate_grad.astype(jnp.bfloat16)
    up_low = up_grad.astype(jnp.bfloat16)
    gate_weight_grad = jnp.einsum("sd,sf->df", inner, gate_low, preferred_element_type=jnp.float32)
    up_weight_grad = jnp.einsum("sd,sf->df", inner, up_low, preferred_element_type=jnp.float32)
    inner_grad = jnp.einsum(
        "sf,df->sd", gate_low, gate_full, preferred_element_type=jnp.float32
    ) + jnp.einsum("sf,df->sd", up_low, up_full, preferred_element_type=jnp.float32)
    middle_part, pre_ffn_gain_grad = pull_pre_ffn(inner_grad)
    middle_grad = upstream + middle_part
    branch_grad, post_attn_gain_grad = pull_post_attn(middle_grad)
    branch_low = branch_grad.astype(jnp.bfloat16)
    o_grad = jnp.einsum("se,sd->ed", attended, branch_low, preferred_element_type=jnp.float32)
    attended_grad = jnp.einsum(
        "sd,ed->se", branch_low, o_full, preferred_element_type=jnp.float32
    ).astype(jnp.bfloat16)
    query_win_grad, key_win_grad, value_win_grad = lax.map(
        attend_backward,
        (
            query_blocks,
            key_windows,
            value_windows,
            place_blocks,
            starts,
            log_totals,
            attended_grad.reshape(blocks, window, -1),
        ),
    )
    queries_grad = query_win_grad.reshape(length, -1)
    keys_grad = fold_windows(key_win_grad, blocks)
    value_low = fold_windows(value_win_grad, blocks).astype(jnp.bfloat16)
    query_raw_grad, query_gain_grad = pull_query(queries_grad)
    key_raw_grad, key_gain_grad = pull_key(keys_grad)
    query_low = query_raw_grad.astype(jnp.bfloat16)
    key_low = key_raw_grad.astype(jnp.bfloat16)
    q_grad = jnp.einsum("sd,se->de", normed, query_low, preferred_element_type=jnp.float32)
    k_grad = jnp.einsum("sd,se->de", normed, key_low, preferred_element_type=jnp.float32)
    v_grad = jnp.einsum("sd,se->de", normed, value_low, preferred_element_type=jnp.float32)
    normed_grad = (
        jnp.einsum("se,de->sd", query_low, q_full, preferred_element_type=jnp.float32)
        + jnp.einsum("se,de->sd", key_low, k_full, preferred_element_type=jnp.float32)
        + jnp.einsum("se,de->sd", value_low, v_full, preferred_element_type=jnp.float32)
    )
    input_part, attn_gain_grad = pull_attn_norm(normed_grad)
    tokens_grad = middle_grad + input_part
    local_grads = (
        q_grad,
        k_grad,
        v_grad,
        o_grad,
        gate_weight_grad,
        up_weight_grad,
        down_grad,
        attn_gain_grad,
        query_gain_grad,
        key_gain_grad,
        post_attn_gain_grad,
        pre_ffn_gain_grad,
        post_ffn_gain_grad,
    )
    owners = lax.axis_size("shard")
    replicas = lax.axis_size("replica")
    packed = pack_owners(local_grads, owners, replicas)
    piece = lax.psum_scatter(packed, ("replica", "shard"), scatter_dimension=0, tiled=True)
    whole = lax.all_gather(piece, "replica", axis=0, tiled=True).reshape(-1)
    summed = unpack_owner(whole, [member.shape for member in owned])
    return (
        mixed,
        tokens_grad,
        summed[0],
        summed[1],
        summed[2],
        summed[3],
        summed[4],
        summed[5],
        summed[6],
        summed[7],
        summed[8],
        summed[9],
        summed[10],
        summed[11],
        summed[12],
    )


def solution(mesh):
    placed = (
        P(("replica", "shard"), None),
        P(("replica", "shard")),
        P(("replica", "shard"), None),
        P("shard", None),
        P("shard", None),
        P("shard", None),
        P("shard", None),
        P("shard", None),
        P("shard", None),
        P("shard", None),
        P("shard"),
        P("shard"),
        P("shard"),
        P("shard"),
        P("shard"),
        P("shard"),
    )
    return jax.shard_map(
        body,
        mesh=mesh,
        in_specs=placed,
        out_specs=(
            P(("replica", "shard"), None),
            P(("replica", "shard"), None),
            P("shard", None),
            P("shard", None),
            P("shard", None),
            P("shard", None),
            P("shard", None),
            P("shard", None),
            P("shard", None),
            P("shard"),
            P("shard"),
            P("shard"),
            P("shard"),
            P("shard"),
            P("shard"),
        ),
        check_vma=False,
    )
```

profile of v0, /device:TPU:0, one launch (start us, length us, event | category | flops | bytes accessed | tf_op | source)
XLA Modules:
  0.0 1109.3 jit_solution(6396285828656181404)
XLA Ops:
  14.8 12.1 %all-reduce.17 = (bf16[640]{0:T(1024)(128)(2,1)S(1)}, bf16[256]{0:T(256)(128)(2,1)S(1)}, bf16[256]{0:T(256)(128)(2,1)S(1)}, bf16[640]{0:T(1024)(128)(2,1)S(1)}, ...) all-reduce(bf16[640]{0:T(1024)(128)(2,1)S(1)} %dynamic-update-slice, ...), channel_id=1, replica_groups=mesh['replica'=8,'shard'=4] {'shard'}, use_global_device_ids=true, to_apply=%add.10 | all-reduce | flops 3072 | bytes 12288
  27.3 9.8 all_gather.44
  46.8 11.0 all_gather.43
  65.0 5.2 multiply_reduce_fusion.2
  70.3 5.2 copy.151
  84.0 4.1 copy.153
  88.0 24.9 %while.30 = (s32[]{:T(128)}, bf16[2,512,1024]{2,1,0:T(8,128)(2,1)}, f32[2,4,512,1]{2,1,3,0:T(4,128)S(1)}, bf16[2,1024,256]{2,1,0:T(8,128)(2,1)S(1)}, s32[2]{0:T(...) while((s32[]{:T(128)}, bf16[2,512,1024]{2,1,0:T(8,128)(2,1)}, ...), condition=%wide.region_6.7_spmd, body=%wide.region_3.6_spmd.sunk | while | flops 2169503232 | bytes 36784292 | solution.py:206
  113.0 3.9 multiply_reduce_fusion.9
  119.8 8.9 fusion.111
  128.7 28.3 %all-gather.14.cloned.1.call-done = bf16[640,2048]{1,0:T(8,128)(2,1)} async-done(((bf16[160,2048]{1,0:T(8,128)(2,1)}), bf16[640,2048]{1,0:T(8,128)(2,1)}) %all-gather.14.cloned.1.call-update) | async-done | bytes 2621456 | tf_op jit(solution)/shard_map/all_gather | solution.py:166
  156.9 11.4 %multiply_convert_fusion.1 = (bf16[1024,2048]{1,0:T(8,128)(2,1)}, f32[1024,2048]{1,0:T(8,128)}) fusion(f32[1024,2048]{1,0:T(8,128)} %fusion.111, bf16[1024,640]{0,1:T(8,128)(2,1)} %multiply_convert_fusion.2, bf16[640,2048]{1,0:T(8,128)(2,1)} %all-gather.14.cloned.1.call-done), kind=kOutput, calls=%fused_computation.77 | convolution fusion | flops 2705326080 | bytes 24903680 | tf_op jit(solution)/shard_map/dot_general | solution.py:216
  168.3 30.0 %all-gather.16.cloned.1.call-done = bf16[2048,640]{1,0:T(8,128)(2,1)} async-done(((bf16[512,640]{1,0:T(8,128)(2,1)}), bf16[2048,640]{1,0:T(8,128)(2,1)}) %all-gather.16.cloned.1.call-update) | async-done | bytes 2621456 | tf_op jit(solution)/shard_map/all_gather | solution.py:167
  198.3 5.7 multiply_reduce_fusion.7
  209.0 12.9 %multiply_convert_fusion = (bf16[1024,2048]{1,0:T(8,128)(2,1)}, bf16[1024,2048]{1,0:T(8,128)(2,1)}) fusion(f32[1024,2048]{1,0:T(8,128)S(1)} %copy-done.76, f32[1024,2048]{1,0:T(8,128)} %get-tuple-element.523, bf16[1024,640]{0,1:T(8,128)(2,1)S(1)} %get-tuple-element.502, bf16[2048,640]{1,0:T(8,128)(2,1)S(1)} %copy-done.66), kind=kOutput, calls=%fused_computation.76 | convolution fusion | flops 2734686208 | bytes 29097984 | tf_op jit(solution)/shard_map/sd,fd->sf/dot_general | solution.py:226
  222.0 4.9 fusion.112
  226.9 3.8 multiply_reduce_fusion.3
  238.3 63.5 %while.31 = (s32[]{:T(128)}, f32[2,512,1024]{1,2,0:T(8,128)}, f32[2,1024,256]{2,1,0:T(8,128)}, f32[2,1024,256]{2,1,0:T(8,128)}, bf16[2,1024,256]{2,1,0:T(8,128)(...) while((s32[]{:T(128)}, f32[2,512,1024]{1,2,0:T(8,128)}, ...), condition=%wide.region_15.16_spmd, body=%wide.region_13.15_spmd.sunk | while | flops 5397020160 | bytes 177809840 | solution.py:243
  239.8 5.5 fusion.199
  251.8 5.0 fusion.201
  271.5 5.5 fusion.199
  283.4 5.0 fusion.201
  308.0 3.5 fusion.115
  311.4 5.1 fusion.116
  316.5 4.7 fusion.117
  321.2 5.2 fusion.118
  329.1 5.4 copy.160
  334.5 5.6 mul.617
  344.0 4.9 multiply_reduce_fusion
  351.3 5.8 fusion.53
  368.5 5.0 reshape.559
  379.0 4.5 reshape.562
  383.5 8.4 reshape.563
  391.9 8.4 reshape.564
  400.2 7.3 reshape.565
  407.5 4.1 fusion.113
  419.5 5.6 constant_dynamic-update-slice_fusion.4
  425.1 5.4 constant_dynamic-update-slice_fusion.3
  441.9 63.8 %reshape.623 = f32[5573632]{0:T(1024)} reshape(f32[4,1393408]{1,0:T(4,128)} %dynamic-update-slice.18) | data formatting | bytes 44589056
  505.6 27.8 %reshape.572 = f32[4,8,174176]{2,1,0:T(8,128)} reshape(f32[5573632]{0:T(1024)} %reshape.623) | data formatting | bytes 44589056 | tf_op jit(solution)/shard_map/reshape | solution.py:114
  533.4 27.4 %copy.169 = f32[8,4,174176]{2,1,0:T(4,128)} copy(f32[8,4,174176]{2,0,1:T(8,128)} %bitcast.240) | data formatting | bytes 44589056 | tf_op jit(solution)/shard_map/transpose | solution.py:114
  560.8 27.6 %reshape.573 = f32[32,174176]{1,0:T(8,128)} reshape(f32[8,4,174176]{2,1,0:T(4,128)} %copy.169) | data formatting | bytes 44589056 | tf_op jit(solution)/shard_map/reshape | solution.py:114
  588.6 356.8 %all-reduce.20.cloned.1.call-done = f32[32,174176]{1,0:T(8,128)} async-done(((f32[32,174176]{1,0:T(8,128)}), f32[32,174176]{1,0:T(8,128)}) %all-reduce.20.cloned.1.call-update) | async-done | bytes 22294544
  945.4 3.6 dynamic-slice_bitcast_fusion.1
  950.5 4.7 fusion.65
  958.5 48.4 %all-gather.18.cloned.1.call-done = f32[8,1,174176]{2,1,0:T(1,128)} async-done(((f32[1,1,174176]{2,1,0:T(1,128)}), f32[8,1,174176]{2,1,0:T(1,128)}) %all-gather.18.cloned.1.call-update) | async-done | bytes 5573648 | tf_op jit(solution)/shard_map/all_gather | solution.py:291
  1006.8 60.3 %reduce.4 = f32[8,174176]{1,0:T(8,128)} reduce(f32[8,1,174176]{2,1,0:T(1,128)} %all-gather.18.cloned.1.call-done, f32[]{:T(128)} %constant.212), dimensions={1}, to_apply=%all-gather.reduce_sub_computation | reduce | bytes 11147268 | tf_op jit(solution)/shard_map/all_gather | solution.py:291
  1067.2 8.1 reshape.574
  1075.2 8.8 slice.108
  (376 shorter events, 184.3 us)
Async XLA Ops:
  7.2 5.5 copy-start.32
  7.2 6.1 copy-start.69
  7.2 6.4 copy-start.70
  7.2 6.6 copy-start.71
  7.2 6.9 copy-start.72
  7.2 7.1 copy-start.73
  7.3 7.3 copy-start.74
  7.3 57.7 %all-gather.8.cloned.1.call-start = ((), (), s32[]{:S(2)}) async-start(), calls=%async_computation | async-start | bytes 1638400 | tf_op jit(solution)/shard_map/all_gather | solution.py:161
  8.0 104.9 %all-gather.10.cloned.1.call-start = ((), (), s32[]{:S(2)}) async-start(), calls=%async_computation.1 | async-start | bytes 1638400 | tf_op jit(solution)/shard_map/all_gather | solution.py:164
  8.7 111.0 %all-gather.12.cloned.1.call-start = ((), (), s32[]{:S(2)}) async-start(), calls=%async_computation.2 | async-start | bytes 3276800 | tf_op jit(solution)/shard_map/all_gather | solution.py:165
  9.5 17.8 %copy-start.38 = (bf16[160,256]{1,0:T(8,128)(2,1)S(1)}, bf16[160,256]{1,0:T(8,128)(2,1)}, u32[]{:S(2)}) copy-start(bf16[160,256]{1,0:T(8,128)(2,1)} %param.24) | copy-start | bytes 245764
  9.5 147.5 %all-gather.14.cloned.1.call-start = ((), (), s32[]{:S(2)}) async-start(), calls=%async_computation.3 | async-start | bytes 3276800 | tf_op jit(solution)/shard_map/all_gather | solution.py:166
  10.1 188.2 %all-gather.16.cloned.1.call-start = ((), (), s32[]{:S(2)}) async-start(), calls=%async_computation.4 | async-start | bytes 3276800 | tf_op jit(solution)/shard_map/all_gather | solution.py:167
  10.7 934.7 %all-reduce.20.cloned.1.call-start = ((), (), s32[]{:S(2)}) async-start(), calls=%async_computation.6 | async-start | bytes 44597248
  10.7 30.4 %copy-start.61 = (f32[128]{0:T(128)}, f32[128]{0:T(128)S(1)}, u32[]{:S(2)}) copy-start(f32[128]{0:T(128)S(1)} %multiply_power_fusion) | copy-start | bytes 1540
  13.3 51.7 %copy-start.1 = (bf16[1024,640]{0,1:T(8,128)(2,1)}, bf16[1024,640]{0,1:T(8,128)(2,1)S(1)}, u32[]{:S(2)}) copy-start(bf16[1024,640]{0,1:T(8,128)(2,1)S(1)} %copy.147) | copy-start | bytes 3932164
  27.0 38.1 %copy-start.46 = (f32[640]{0:T(1024)}, f32[640]{0:T(1024)S(1)}, u32[]{:S(2)}) copy-start(f32[640]{0:T(1024)S(1)} %convert_element_type.124) | copy-start | bytes 7684
  27.0 10.9 copy-start.55
  27.3 11.4 %copy-start.50 = (f32[1024]{0:T(1024)}, f32[1024]{0:T(1024)S(1)}, u32[]{:S(2)}) copy-start(f32[1024]{0:T(1024)S(1)} %fusion.66) | copy-start | bytes 12292
  27.3 37.7 %copy-start.48 = (f32[1024]{0:T(1024)}, f32[1024]{0:T(1024)S(1)}, u32[]{:S(2)}) copy-start(f32[1024]{0:T(1024)S(1)} %fusion.86) | copy-start | bytes 12292
  41.1 5.7 copy-start.39
  44.1 34.7 %copy-start.16 = (f32[1024,128]{1,0:T(8,128)}, f32[1024,128]{1,0:T(8,128)S(1)}, u32[]{:S(2)}) copy-start(f32[1024,128]{1,0:T(8,128)S(1)} %get-tuple-element.514) | copy-start | bytes 1572868
  62.3 13.5 %copy-start.59 = (f32[256]{0:T(256)}, f32[256]{0:T(256)S(1)}, u32[]{:S(2)}) copy-start(f32[256]{0:T(256)S(1)} %convert_element_type.133) | copy-start | bytes 3076
  70.3 5.2 copy-start.44
  112.9 4.0 copy-start.9
  112.9 4.0 copy-start.2
  198.3 5.7 copy-start.7
  207.5 14.4 %copy-start.30 = (bf16[1024,640]{0,1:T(8,128)(2,1)}, bf16[1024,640]{0,1:T(8,128)(2,1)S(1)}, u32[]{:S(2)}) copy-start(bf16[1024,640]{0,1:T(8,128)(2,1)S(1)} %get-tuple-element.502) | copy-start | bytes 3932164
  209.0 12.9 %copy-start.64 = (bf16[640,2048]{1,0:T(8,128)(2,1)S(1)}, bf16[640,2048]{1,0:T(8,128)(2,1)}, u32[]{:S(2)}) copy-start(bf16[640,2048]{1,0:T(8,128)(2,1)} %all-gather.12.cloned.1.call-done) | copy-start | bytes 7864324
  222.0 4.9 copy-start.65
  222.0 4.9 copy-start.77
  251.8 5.1 slice-start
  251.8 6.1 slice-start.1
  283.4 5.1 slice-start
  283.4 6.1 slice-start.1
  311.4 5.1 copy-start.78
  316.5 4.7 copy-start.31
  316.5 4.7 copy-start.80
  321.2 5.2 copy-start.20
  343.4 5.6 copy-start.8
  344.0 6.2 copy-start.45
  407.5 4.1 copy-start.10
  407.5 4.1 copy-start.29
  419.5 11.1 slice-start.2
  425.1 5.4 slice-start.3
  588.5 360.5 %copy-start.15 = (bf16[1024,640]{0,1:T(8,128)(2,1)S(1)}, bf16[1024,640]{0,1:T(8,128)(2,1)}, u32[]{:S(2)}) copy-start(bf16[1024,640]{0,1:T(8,128)(2,1)} %get-tuple-element.503) | copy-start | bytes 3932164
  588.5 361.9 %copy-start.51 = (f32[1024]{0:T(1024)S(1)}, f32[1024]{0:T(1024)}, u32[]{:S(2)}) copy-start(f32[1024]{0:T(1024)} %copy-done.50) | copy-start | bytes 12292
  588.5 418.3 %all-gather.18.cloned.1.call-start = ((), (), s32[]{:S(2)}) async-start(), calls=%async_computation.5 | async-start | bytes 6271488 | tf_op jit(solution)/shard_map/all_gather | solution.py:291
  (52 other events, 136.6 us)
Sparse Core Ops, SparseCore 0:
  9.9 32.5 all-gather.7
  44.3 29.6 all-gather.9
  75.9 39.6 all-gather.11
  117.3 39.6 all-gather.13
  158.6 39.6 all-gather.15
  588.6 356.7 all-reduce.19
  949.1 57.6 all-gather.17
where the time goes:
time: 1120 us; the launch traced here: 1110 us
  waiting for transfers between devices  467 us (42%)
  local copies, waits for them, and re-layouts  333 us (30%)
  matrix products  136 us (12%)
  other arithmetic  120 us (11%)
  blocking collectives  32.9 us (3%)
  between operations  16.7 us (1%)
    unnamed x8, waiting for transfers between devices  360 us
    unnamed x188, local copies, waits for them, and re-layouts  118 us
    all_gather x1, other arithmetic, body(): whole = lax.all_gather(piece, 'replica', axis=0, tiled=True).reshape(-1)  60.3 us
    reshape x2, local copies, waits for them, and re-layouts, pack_owners(): flattened.reshape(owners, replicas, -1).transpose(1, 0, 2)  55.4 us
    all_gather x1, waiting for transfers between devices, body(): whole = lax.all_gather(piece, 'replica', axis=0, tiled=True).reshape(-1)  48.4 us
    reshape x13, local copies, waits for them, and re-layouts, pack_owners(): member.reshape(owners, -1)  35.7 us
    all_gather x1, waiting for transfers between devices, body(): lax.all_gather(down_weight, 'shard', axis=0, tiled=True)  30 us
    all_gather x1, waiting for transfers between devices, body(): lax.all_gather(up_weight, 'shard', axis=0, tiled=True)  28.3 us
  transfers between devices with their start and end apart: 7, of which 4 were waited for; matrix products, arithmetic and copies ran while one was open for 9% of the time, Pallas kernels for 0%

commit v1 on v0

v1 whole, which is shorter than its diff:
```python
import jax
import jax.numpy as jnp
from jax import lax
from jax.experimental import pallas as pl
from jax.experimental.pallas import tpu as pltpu
from jax.sharding import PartitionSpec as P

HEAD = 256
WINDOW = 512


EPSILON = 1e-06


def rms_scale(values, scale_gain):
    return (
        values * lax.rsqrt(jnp.mean(values * values, axis=-1, keepdims=True) + EPSILON) * scale_gain
    )


def rotary_angles(positions, head_width):
    indices = jnp.arange(head_width // 2).astype(jnp.float32)
    frequency = 10000.0 ** (-2.0 * indices / head_width)
    return positions.astype(jnp.float32)[:, None] * frequency[None, :]


def visible_keys(start, first, query_pos):
    shape = (WINDOW, start + WINDOW - first)
    row_index = start + lax.broadcasted_iota(jnp.int32, shape, 0)
    col_index = first + lax.broadcasted_iota(jnp.int32, shape, 1)
    distance = row_index - col_index
    return (distance >= 0) & (distance < WINDOW) & (distance <= query_pos)


def kernel_dot(left, right, dims):
    return lax.dot_general(left, right, (dims, ((), ())), preferred_element_type=jnp.float32)


def forward_kernel(query_ref, key_ref, value_ref, place_ref, out_ref, total_ref):
    for start in range(0, query_ref.shape[0], WINDOW):
        first = max(0, start - WINDOW)
        own = pl.ds(start, WINDOW)
        span = pl.ds(first, start + WINDOW - first)
        scores = kernel_dot(query_ref[own, :], key_ref[span, :], ((1,), (1,)))
        seen = visible_keys(start, first, place_ref[own, :])
        scores = jnp.where(seen, scores, -1e30)
        highest = jnp.max(scores, axis=-1, keepdims=True)
        raised = jnp.exp(scores - highest)
        summed = jnp.sum(raised, axis=-1, keepdims=True)
        shares = (raised / summed).astype(jnp.bfloat16)
        out_ref[own, :] = kernel_dot(shares, value_ref[span, :], ((1,), (0,))).astype(
            jnp.bfloat16
        )
        total_ref[0, own, :] = highest + jnp.log(summed)


def backward_kernel(
    query_ref,
    key_ref,
    value_ref,
    place_ref,
    total_ref,
    out_grad_ref,
    query_grad_ref,
    key_grad_ref,
    value_grad_ref,
):
    @pl.when(pl.program_id(0) == 0)
    def _():
        key_grad_ref[...] = jnp.zeros_like(key_grad_ref)
        value_grad_ref[...] = jnp.zeros_like(value_grad_ref)

    for start in range(0, query_ref.shape[0], WINDOW):
        first = max(0, start - WINDOW)
        own = pl.ds(start, WINDOW)
        span = pl.ds(first, start + WINDOW - first)
        queries = query_ref[own, :]
        out_grad = out_grad_ref[own, :]
        key_rows = key_ref[span, :]
        scores = kernel_dot(queries, key_rows, ((1,), (1,)))
        seen = visible_keys(start, first, place_ref[own, :])
        shares = jnp.where(seen, jnp.exp(scores - total_ref[0, own, :]), 0.0)
        share_grad = kernel_dot(out_grad, value_ref[span, :], ((1,), (1,)))
        spread = jnp.sum(shares * share_grad, axis=-1, keepdims=True)
        scores_low = (shares * (share_grad - spread)).astype(jnp.bfloat16)
        query_grad_ref[own, :] = kernel_dot(scores_low, key_rows, ((1,), (0,)))
        key_grad_ref[span, :] += kernel_dot(scores_low, queries, ((0,), (0,)))
        value_grad_ref[span, :] += kernel_dot(shares.astype(jnp.bfloat16), out_grad, ((0,), (0,)))


def attention_specs(length):
    by_head = pl.BlockSpec((length, HEAD), lambda h: (0, h))
    shared = pl.BlockSpec((length, HEAD), lambda h: (0, 0))
    place = pl.BlockSpec((length, 1), lambda h: (0, 0))
    total = pl.BlockSpec((1, length, 1), lambda h: (h, 0, 0))
    return (by_head, shared, place, total)


def attention_forward(queries, key_rows, values, positions):
    length, columns = queries.shape
    heads = columns // HEAD
    by_head, shared, place, total = attention_specs(length)
    return pl.pallas_call(
        forward_kernel,
        grid=(heads,),
        in_specs=[by_head, shared, shared, place],
        out_specs=[by_head, total],
        out_shape=[
            jax.ShapeDtypeStruct((length, columns), jnp.bfloat16),
            jax.ShapeDtypeStruct((heads, length, 1), jnp.float32),
        ],
        compiler_params=pltpu.CompilerParams(vmem_limit_bytes=40 * 2**20),
        cost_estimate=pl.CostEstimate(
            flops=6 * length * WINDOW * columns,
            bytes_accessed=6 * length * columns,
            transcendentals=2 * length * WINDOW * heads,
        ),
        name="attention_forward",
    )(queries, key_rows, values, positions[:, None])


def attention_backward(queries, key_rows, values, positions, totals, out_grad):
    length, columns = queries.shape
    heads = columns // HEAD
    by_head, shared, place, total = attention_specs(length)
    return pl.pallas_call(
        backward_kernel,
        grid=(heads,),
        in_specs=[by_head, shared, shared, place, total, by_head],
        out_specs=[by_head, shared, shared],
        out_shape=[
            jax.ShapeDtypeStruct((length, columns), jnp.float32),
            jax.ShapeDtypeStruct((length, HEAD), jnp.float32),
            jax.ShapeDtypeStruct((length, HEAD), jnp.float32),
        ],
        compiler_params=pltpu.CompilerParams(vmem_limit_bytes=40 * 2**20),
        cost_estimate=pl.CostEstimate(
            flops=15 * length * WINDOW * columns,
            bytes_accessed=12 * length * columns,
            transcendentals=2 * length * WINDOW * heads,
        ),
        name="attention_backward",
    )(queries, key_rows, values, positions[:, None], totals, out_grad)


def gelu_product(gate, upward):
    return jax.nn.gelu(gate, approximate=True) * upward


def rope_pair(values, cosine, sine_part):
    half_width = values.shape[-1] // 2
    front_half = values[..., :half_width]
    back_half = values[..., half_width:]
    return jnp.concatenate(
        [front_half * cosine - back_half * sine_part, back_half * cosine + front_half * sine_part],
        axis=-1,
    )


def swap_cores(member):
    return lax.ppermute(member, "core", [(0, 1), (1, 0)])


def in_core_order(mine, other, core, axis):
    first = jnp.where(core == 0, mine, other)
    second = jnp.where(core == 0, other, mine)
    return jnp.stack([first, second], axis=axis)


def halve_over_owners(member, shard, owners, low_first):
    bits = owners.bit_length() - 1
    pieces = member.reshape((2,) * bits + member.shape[1:])
    left = list(range(bits - 1, -1, -1))
    while left:
        place = len(left) - 1 if low_first else 0
        bit = left.pop(place)
        mine = (shard >> bit) & 1
        sent = lax.dynamic_index_in_dim(pieces, 1 - mine, place, keepdims=False)
        kept = lax.dynamic_index_in_dim(pieces, mine, place, keepdims=False)
        pairs = [(device, device ^ (1 << bit)) for device in range(owners)]
        pieces = kept + lax.ppermute(sent, "shard", pairs)
    return pieces


def reduce_pair(other, mine, shard, owners, low_first):
    paired = mine + swap_cores(other)
    piece = halve_over_owners(paired, shard, owners, low_first)
    return lax.psum(piece, "z")


def body(
    tokens,
    positions,
    cotangent,
    q_weight,
    k_weight,
    v_weight,
    o_weight,
    gate_weight,
    up_weight,
    down_weight,
    attn_gain,
    query_gain,
    key_gain,
    post_attn_gain,
    pre_ffn_gain,
    post_ffn_gain,
):
    core = lax.axis_index("core")
    shard = lax.axis_index("shard")
    owners = lax.axis_size("shard")
    f32 = jnp.float32
    low = jnp.bfloat16
    width = tokens.shape[1]
    length = tokens.shape[0]

    def dot(left, right, dims):
        return lax.dot_general(left, right, (dims, ((), ())), preferred_element_type=f32)

    def gather(half):
        mine = lax.all_gather(half, "shard", axis=0, tiled=False)
        return mine, swap_cores(mine)

    gains = (attn_gain, query_gain, key_gain, post_attn_gain, pre_ffn_gain, post_ffn_gain)
    gain_sizes = [member.shape[0] for member in gains]
    gain_line = jnp.concatenate(gains)
    qkv_weight = jnp.concatenate([q_weight, k_weight, v_weight], axis=1)
    rows, columns = qkv_weight.shape
    gain_rows = -(-gain_line.shape[0] // columns)
    pad_rows = -(-gain_rows // 16) * 16
    gain_block = jnp.pad(gain_line, (0, pad_rows * columns - gain_line.shape[0]))
    gain_block = gain_block.reshape(pad_rows, columns)
    qkv_half = lax.dynamic_index_in_dim(
        qkv_weight.reshape(2, rows // 2, columns), core, 0, keepdims=False
    )
    qkv_mine, qkv_other = gather(jnp.concatenate([qkv_half, gain_block], axis=0))
    gain_all = qkv_mine[:, rows // 2 : rows // 2 + gain_rows].reshape(owners, -1)
    split_gains = []
    offset = 0
    for size in gain_sizes:
        split_gains.append(gain_all[:, offset : offset + size].reshape(-1).astype(f32))
        offset += size
    gain_attn, gain_query, gain_key, gain_post_attn, gain_pre_ffn, gain_post_ffn = split_gains
    qkv_full = in_core_order(
        qkv_mine[:, : rows // 2], qkv_other[:, : rows // 2], core, 1
    ).reshape(owners * rows, columns)

    o_rows = o_weight.shape[0]
    o_half = lax.dynamic_index_in_dim(
        o_weight.reshape(2, o_rows // 2, width), core, 0, keepdims=False
    )
    o_mine, o_other = gather(o_half)
    o_full = in_core_order(o_mine, o_other, core, 1).reshape(owners * o_rows, width)

    unit_half = down_weight.shape[0] // 2

    def unit_columns(member):
        shaped = member.reshape(member.shape[0], owners, 2, unit_half)
        return lax.dynamic_index_in_dim(shaped, core, 2, keepdims=False).reshape(
            member.shape[0], owners * unit_half
        )

    def flat_rows(pair):
        return tuple(member.reshape(-1, member.shape[-1]) for member in pair)

    gate_pair = flat_rows(gather(unit_columns(gate_weight)))
    up_pair = flat_rows(gather(unit_columns(up_weight)))
    down_pair = flat_rows(
        gather(
            lax.dynamic_index_in_dim(
                down_weight.reshape(2, unit_half, width), core, 0, keepdims=False
            )
        )
    )

    window = WINDOW
    blocks = length // window
    inputs = tokens.astype(f32)
    angles = rotary_angles(positions, HEAD)
    cosine = jnp.cos(angles)
    sine_part = jnp.sin(angles)
    normed_f, pull_attn_norm = jax.vjp(rms_scale, inputs, gain_attn)
    normed = normed_f.astype(low)
    q_cols = q_weight.shape[1]
    heads = q_cols // HEAD
    qkv_raw = dot(normed, qkv_full, ((1,), (0,)))
    values = qkv_raw[:, q_cols + HEAD :].astype(low)

    def prepare(raw_rows, scale_gain, factor):
        return rope_pair(rms_scale(raw_rows, scale_gain), cosine, sine_part) * factor

    def prepare_queries(raw_rows, scale_gain):
        return [
            prepare(raw_rows[:, h * HEAD : (h + 1) * HEAD], scale_gain, HEAD ** (-0.5))
            for h in range(heads)
        ]

    queries_f, pull_query = jax.vjp(prepare_queries, qkv_raw[:, :q_cols], gain_query)
    key_f, pull_key = jax.vjp(
        lambda raw_rows, scale_gain: prepare(raw_rows, scale_gain, 1.0),
        qkv_raw[:, q_cols : q_cols + HEAD],
        gain_key,
    )
    queries = jnp.concatenate([member.astype(low) for member in queries_f], axis=1)
    key_rows = key_f.astype(low)
    attended, log_totals = attention_forward(queries, key_rows, values, positions)
    branch = dot(attended, o_full, ((1,), (0,)))
    post_attn_f, pull_post_attn = jax.vjp(rms_scale, branch, gain_post_attn)
    middle = inputs + post_attn_f
    inner_f, pull_pre_ffn = jax.vjp(rms_scale, middle, gain_pre_ffn)
    inner = inner_f.astype(low)
    gates = [dot(inner, member, ((1,), (0,))) for member in gate_pair]
    ups = [dot(inner, member, ((1,), (0,))) for member in up_pair]
    hiddens, pulls = [], []
    for gate, upward in zip(gates, ups):
        hidden_f, pull_glu = jax.vjp(gelu_product, gate, upward)
        hiddens.append(hidden_f.astype(low))
        pulls.append(pull_glu)
    ffn_out = dot(hiddens[0], down_pair[0], ((1,), (0,))) + dot(
        hiddens[1], down_pair[1], ((1,), (0,))
    )
    post_ffn_f, pull_post_ffn = jax.vjp(rms_scale, ffn_out, gain_post_ffn)
    mixed = (middle + post_ffn_f).astype(low)
    upstream = cotangent.astype(f32)
    ffn_grad, post_ffn_gain_grad = pull_post_ffn(upstream)
    ffn_low = ffn_grad.astype(low)

    down_other = dot(hiddens[1], ffn_low, ((0,), (0,))).reshape(owners, unit_half, width)
    down_mine = dot(hiddens[0], ffn_low, ((0,), (0,))).reshape(owners, unit_half, width)
    ffn_low, down_other, down_mine = lax.optimization_barrier((ffn_low, down_other, down_mine))
    down_sum = reduce_pair(down_other, down_mine, shard, owners, False)
    gate_lows, up_lows = [], []
    for pull_glu, down_half in zip(pulls, down_pair):
        hidden_grad = dot(ffn_low, down_half, ((1,), (1,)))
        gate_grad, up_grad = pull_glu(hidden_grad)
        gate_lows.append(gate_grad.astype(low))
        up_lows.append(up_grad.astype(low))
    owner_rows = gate_weight.shape[0]
    gate_other = dot(inner, gate_lows[1], ((0,), (0,))).reshape(owners, owner_rows, -1)
    gate_mine = dot(inner, gate_lows[0], ((0,), (0,))).reshape(owners, owner_rows, -1)
    up_other = dot(inner, up_lows[1], ((0,), (0,))).reshape(owners, owner_rows, -1)
    up_mine = dot(inner, up_lows[0], ((0,), (0,))).reshape(owners, owner_rows, -1)
    gate_lows[0], gate_other, gate_mine, up_other, up_mine = lax.optimization_barrier(
        (gate_lows[0], gate_other, gate_mine, up_other, up_mine)
    )
    gate_sum = reduce_pair(gate_other, gate_mine, shard, owners, True)
    up_sum = reduce_pair(up_other, up_mine, shard, owners, False)
    inner_grad = (
        dot(gate_lows[0], gate_pair[0], ((1,), (1,)))
        + dot(gate_lows[1], gate_pair[1], ((1,), (1,)))
        + dot(up_lows[0], up_pair[0], ((1,), (1,)))
        + dot(up_lows[1], up_pair[1], ((1,), (1,)))
    )
    middle_part, pre_ffn_gain_grad = pull_pre_ffn(inner_grad)
    middle_grad = upstream + middle_part
    branch_grad, post_attn_gain_grad = pull_post_attn(middle_grad)
    branch_low = branch_grad.astype(low)
    attended_parts = attended.reshape(length, owners, 2, o_rows // 2)

    def o_part(which):
        rows_of = lax.dynamic_index_in_dim(attended_parts, which, 2, keepdims=False)
        return dot(rows_of.reshape(length, -1), branch_low, ((0,), (0,))).reshape(
            owners, o_rows // 2, width
        )

    o_other, o_mine = o_part(1 - core), o_part(core)
    branch_low, o_other, o_mine = lax.optimization_barrier((branch_low, o_other, o_mine))
    o_sum = reduce_pair(o_other, o_mine, shard, owners, True)
    attended_grad = dot(branch_low, o_full, ((1,), (1,))).astype(low)
    queries_grad, keys_grad, value_grad = attention_backward(
        queries, key_rows, values, positions, log_totals, attended_grad
    )
    value_low = value_grad.astype(low)
    query_raw_grad, query_gain_grad = pull_query(
        [queries_grad[:, h * HEAD : (h + 1) * HEAD] for h in range(heads)]
    )
    key_raw_grad, key_gain_grad = pull_key(keys_grad)
    qkv_low = jnp.concatenate(
        [query_raw_grad.astype(low), key_raw_grad.astype(low), value_low], axis=1
    )
    half_columns = columns // 2

    def qkv_part(which):
        picked = lax.dynamic_slice_in_dim(qkv_low, which * half_columns, half_columns, 1)
        return dot(normed, picked, ((0,), (0,))).reshape(owners, rows, half_columns)

    qkv_other, qkv_mine = qkv_part(1 - core), qkv_part(core)
    qkv_low, qkv_other, qkv_mine = lax.optimization_barrier((qkv_low, qkv_other, qkv_mine))
    qkv_sum = reduce_pair(qkv_other, qkv_mine, shard, owners, False)
    normed_grad = dot(qkv_low, qkv_full, ((1,), (1,)))
    input_part, attn_gain_grad = pull_attn_norm(normed_grad)
    tokens_grad = middle_grad + input_part
    gain_grads = jnp.concatenate(
        [
            attn_gain_grad,
            query_gain_grad,
            key_gain_grad,
            post_attn_gain_grad,
            pre_ffn_gain_grad,
            post_ffn_gain_grad,
        ]
    )
    gain_sum = lax.psum(gain_grads, ("z", "core", "shard"))
    gain_outs = []
    offset = 0
    for size in gain_sizes:
        gain_outs.append(lax.dynamic_slice_in_dim(gain_sum, offset + shard * size, size, 0))
        offset += size * owners

    def finish(member, axis):
        return in_core_order(member, swap_cores(member), core, axis)

    down_out = finish(down_sum, 0).reshape(2 * unit_half, width)
    gate_out = finish(gate_sum.reshape(owner_rows, owners, unit_half), 2)
    up_out = finish(up_sum.reshape(owner_rows, owners, unit_half), 2)
    o_out = finish(o_sum, 0).reshape(o_rows, width)
    qkv_out = finish(qkv_sum, 1).reshape(rows, columns)
    return (
        mixed,
        tokens_grad,
        qkv_out[:, :q_cols],
        qkv_out[:, q_cols : q_cols + HEAD],
        qkv_out[:, q_cols + HEAD :],
        o_out,
        gate_out.reshape(owner_rows, -1),
        up_out.reshape(owner_rows, -1),
        down_out,
        *gain_outs,
    )


def solution(mesh):
    replicas = mesh.shape["replica"]
    owners = mesh.shape["shard"]
    split = jax.sharding.Mesh(
        mesh.devices.reshape(replicas // 2, 2, owners), ("z", "core", "shard")
    )
    every = ("z", "core", "shard")
    weights = [P("shard", None)] * 7
    gains = [P("shard")] * 6
    return jax.shard_map(
        body,
        mesh=split,
        in_specs=(P(every, None), P(every), P(every, None), *weights, *gains),
        out_specs=(P(every, None), P(every, None), *weights, *gains),
        check_vma=False,
    )
```

time: 1120 us -> 606 us (0.54)
  local copies, waits for them, and re-layouts: 333 us -> 76.4 us
  waiting for transfers between devices: 467 us -> 274 us
  other arithmetic: 120 us -> 60.9 us
  matrix products: 136 us -> 84.9 us
  Pallas kernels: 0 us -> 21.4 us
  blocking collectives: 32.9 us -> 53.9 us
  starting transfers between devices: 0.27 us -> 13.3 us
    unnamed x8 -> x5, waiting for transfers between devices: 360 us -> 0.08 us
    reshape x23 -> x8, local copies, waits for them, and re-layouts: 112 us -> 12.3 us  [the longest x1 4.84 us: body(): attended_parts = attended.reshape(length, owners, 2, o_rows // 2)]
    psum x0 -> x1, waiting for transfers between devices: none -> 99 us  [reduce_pair(): return lax.psum(piece, 'z')]
    unnamed x188 -> x118, local copies, waits for them, and re-layouts: 118 us -> 34 us
    ppermute x0 -> x25, waiting for transfers between devices: none -> 79 us  [the longest x10 70 us: halve_over_owners(): pieces = kept + lax.ppermute(sent, 'shard', pairs)]
    all_gather x1 -> x0, other arithmetic: 60.3 us -> none  [body(): whole = lax.all_gather(piece, 'replica', axis=0, tiled=True).reshape(-1)]
    dot_general x35 -> x26, matrix products: 136 us -> 84.9 us  [dot(): lax.dot_general(left, right, (dims, ((), ())), preferred_element_type=f32)]
    psum x0 -> x1, blocking collectives: none -> 39.5 us  [body(): gain_sum = lax.psum(gain_grads, ('z', 'core', 'shard'))]
  transfers between devices with their start and end apart: 7 -> 30, of which waited for: 4 -> 13; matrix products, arithmetic and copies ran while one was open for 9% -> 23% of each run, Pallas kernels for 0% -> 2%
where the time goes in v1:
time: 606 us; the launch traced here: 600 us
  waiting for transfers between devices  274 us (45%)
  matrix products  84.9 us (14%)
  local copies, waits for them, and re-layouts  76.4 us (13%)
  other arithmetic  60.9 us (10%)
  blocking collectives  53.9 us (9%)
  Pallas kernels  21.4 us (4%)
  between operations  15.3 us (3%)
  starting transfers between devices  13.3 us (2%)
    psum x1, waiting for transfers between devices, reduce_pair(): return lax.psum(piece, 'z')  99 us
    all_gather x4, waiting for transfers between devices, gather(): mine = lax.all_gather(half, 'shard', axis=0, tiled=False)  95.9 us
    dot_general x26, matrix products, dot(): lax.dot_general(left, right, (dims, ((), ())), preferred_element_type=f32)  84.9 us
    ppermute x10, waiting for transfers between devices, halve_over_owners(): pieces = kept + lax.ppermute(sent, 'shard', pairs)  70 us
    psum x1, blocking collectives, body(): gain_sum = lax.psum(gain_grads, ('z', 'core', 'shard'))  39.5 us
    unnamed x118, local copies, waits for them, and re-layouts  34 us
    all_gather x1, blocking collectives, gather(): mine = lax.all_gather(half, 'shard', axis=0, tiled=False)  14.4 us
  transfers between devices with their start and end apart: 30, of which 13 were waited for; matrix products, arithmetic and copies ran while one was open for 23% of the time, Pallas kernels for 2%

profile of v1, /device:TPU:0, one launch (start us, length us, event | category | flops | bytes accessed | tf_op | source)
XLA Modules:
  0.0 599.9 jit_solution(15555216083083078196)
XLA Ops:
  7.3 4.2 concatenate.35
  21.6 14.4 %all_gather.22 = bf16[4,128,640]{2,1,0:T(8,128)(2,1)S(1)} all-gather(bf16[1,128,640]{2,1,0:T(8,128)(2,1)S(1)} %constant_dynamic-slice_fusion.3), channel_id=1, replica_groups=mesh['z'=4,'core'=2,'shard'=4] {'shard'}, dimensions={0}, use_global_device_ids=true | all-gather | bytes 819200 | tf_op jit(solution)/shard_map/all_gather | solution.py:221
  36.0 2.4 copy.75
  40.6 5.2 all-gather.12.cloned.1.call-done
  48.8 28.3 %all-gather.6.cloned.1.call-done = bf16[4,160,1024]{2,1,0:T(8,128)(2,1)} async-done(((bf16[1,160,1024]{2,1,0:T(8,128)(2,1)}), bf16[4,160,1024]{2,1,0:T(8,128)(2,1)}) %all-gather.6.cloned.1.call-update) | async-done | bytes 1310736 | tf_op jit(solution)/shard_map/all_gather | solution.py:221
  77.1 31.3 %all-gather.8.cloned.1.call-done = bf16[4,160,1024]{2,1,0:T(8,128)(2,1)} async-done(((bf16[1,160,1024]{2,1,0:T(8,128)(2,1)}), bf16[4,160,1024]{2,1,0:T(8,128)(2,1)}) %all-gather.8.cloned.1.call-update) | async-done | bytes 1310736 | tf_op jit(solution)/shard_map/all_gather | solution.py:221
  108.4 31.1 %all-gather.10.cloned.1.call-done = bf16[4,256,640]{2,1,0:T(8,128)(2,1)} async-done(((bf16[1,256,640]{2,1,0:T(8,128)(2,1)}), bf16[4,256,640]{2,1,0:T(8,128)(2,1)}) %all-gather.10.cloned.1.call-update) | async-done | bytes 1310736 | tf_op jit(solution)/shard_map/all_gather | solution.py:221
  141.3 2.8 fusion.117
  150.0 2.7 fusion.91
  153.3 9.3 %attention_forward.1 = (bf16[1024,1024]{1,0:T(8,128)(2,1)S(1)}, f32[4,1024,1]{2,1,0:T(8,128)S(1)}) custom-call(bf16[1024,1024]{1,0:T(8,128)(2,1)S(1)} %pad_maximum_fusion.1.query_ref, bf16[1024,256]{1,0:T(8,128)(2,1)S(1)} %pad_maximum_fusion.9.key_ref, bf16[1024,256]{1,0:T(8,128)(2,1)S(1)} %slice.222.value_ref, s32[1024,1]{1,0:T(8,128)S(1)} %copy.71.place_ref), custom_call_target="tpu_custom_call" | custom-call | flops 3221225472 | bytes 6291456 | tf_op jit(solution)/shard_map/attention_forward/pallas_call | solution.py:103
  165.2 4.8 reshape.399
  170.1 3.7 multiply_reduce_fusion.6
  176.5 6.4 %constant_dynamic-slice_fusion = (bf16[1024,4,1,128]{3,2,1,0:T(2,128)(2,1)}, bf16[1024,4,1,128]{3,2,1,0:T(2,128)(2,1)}) fusion(bf16[1024,4,2,128]{3,2,1,0:T(2,128)(2,1)S(1)} %copy-done.18, s32[]{:T(128)S(6)} %select_n.157, s32[]{:T(128)S(6)} %select_n.164), kind=kLoop, calls=%fused_computation.232 | loop fusion | bytes 4194312 | tf_op jit(solution)/shard_map/jit(dynamic_index_in_dim)/dynamic_slice | solution.py:361
  184.4 3.9 fusion.122
  188.3 5.8 copy.104
  194.2 5.8 copy.105
  200.0 6.0 multiply_convert_fusion.3
  207.6 3.2 fusion.124
  210.8 4.1 multiply_convert_fusion.2
  214.9 3.1 multiply_reduce_fusion.4
  221.8 3.3 fusion.125
  225.2 3.5 fusion.126
  228.6 4.8 fusion.6
  235.0 3.1 fusion.130
  238.1 6.3 %multiply_convert_fusion.1 = (bf16[1024,1024]{1,0:T(8,128)(2,1)S(1)}, bf16[1024,1024]{1,0:T(8,128)(2,1)S(1)}) fusion(f32[1024,1024]{1,0:T(8,128)S(1)} %fusion.124, f32[1024,1024]{1,0:T(8,128)S(1)} %get-tuple-element.220, bf16[1024,640]{0,1:T(8,128)(2,1)S(1)} %get-tuple-element.35, bf16[1024,640]{1,0:T(8,128)(2,1)} %bitcast.19), kind=kOutput, calls=%fused_computation.25 | convolution fusion | flops 1367343104 | bytes 15204352 | tf_op jit(solution)/shard_map/dot_general | solution.py:218
  244.4 3.0 fusion.127
  247.5 2.9 fusion.132
  250.3 3.0 fusion.128
  253.4 3.0 fusion.129
  258.0 3.9 multiply_reduce_fusion
  271.9 12.0 %attention_backward.1 = (f32[1024,1024]{1,0:T(8,128)S(1)}, f32[1024,256]{1,0:T(8,128)S(1)}, f32[1024,256]{1,0:T(8,128)S(1)}) custom-call(bf16[1024,1024]{1,0:T(8,128)(2,1)S(1)} %pad_maximum_fusion.1.query_ref, bf16[1024,256]{1,0:T(8,128)(2,1)S(1)} %pad_maximum_fusion.9.key_ref, bf16[1024,256]{1,0:T(8,128)(2,1)S(1)} %copy-done.4, ...), custom_call_target="tpu_custom_call" | custom-call | flops 8053063680 | bytes 12582912 | tf_op jit(solution)/shard_map/attention_backward/pallas_call | solution.py:126
  284.4 2.7 fusion.94
  296.2 2.5 fusion.29
  298.7 2.5 fusion.27
  302.2 8.9 %collective-permute-done.9 = f32[4,128,640]{2,1,0:T(8,128)} collective-permute-done((f32[4,128,640]{2,1,0:T(8,128)}, f32[4,128,640]{2,1,0:T(8,128)}, u32[]{:S(2)}, u32[]{:S(2)}) %collective-permute-start.9) | collective-permute-done | bytes 1310752 | tf_op jit(solution)/shard_map/ppermute | solution.py:161
  314.6 2.5 add.350
  318.8 2.3 add.360
  323.8 7.0 %collective-permute-done.10 = f32[2,128,640]{2,1,0:T(8,128)} collective-permute-done((f32[2,128,640]{2,1,0:T(8,128)S(1)}, f32[2,128,640]{2,1,0:T(8,128)}, u32[]{:S(2)}, u32[]{:S(2)}) %collective-permute-start.10) | collective-permute-done | bytes 655392 | tf_op jit(solution)/shard_map/ppermute | solution.py:181
  338.7 2.8 add.366
  343.1 7.0 %collective-permute-done.11 = f32[128,640]{1,0:T(8,128)} collective-permute-done((f32[128,640]{1,0:T(8,128)}, f32[128,640]{1,0:T(8,128)}, u32[]{:S(2)}, u32[]{:S(2)}) %collective-permute-start.11) | collective-permute-done | bytes 327712 | tf_op jit(solution)/shard_map/ppermute | solution.py:181
  354.0 4.9 collective-permute-done.14
  362.0 16.2 %collective-permute-done.18 = f32[2,160,1024]{2,1,0:T(8,128)} collective-permute-done((f32[2,160,1024]{2,1,0:T(8,128)S(1)}, f32[2,160,1024]{2,1,0:T(8,128)}, u32[]{:S(2)}, u32[]{:S(2)}) %collective-permute-start.18) | collective-permute-done | bytes 1310752 | tf_op jit(solution)/shard_map/ppermute | solution.py:181
  381.3 25.0 %collective-permute-done.22 = f32[2,256,640]{2,1,0:T(8,128)S(1)} collective-permute-done((f32[2,256,640]{2,1,0:T(8,128)S(1)}, f32[2,256,640]{2,1,0:T(8,128)S(1)}, u32[]{:S(2)}, u32[]{:S(2)}) %collective-permute-start.22) | collective-permute-done | bytes 1310752 | tf_op jit(solution)/shard_map/ppermute | solution.py:181
  409.8 9.4 %collective-permute-done.15 = f32[160,1024]{1,0:T(8,128)S(1)} collective-permute-done((f32[160,1024]{1,0:T(8,128)S(1)}, f32[160,1024]{1,0:T(8,128)S(1)}, u32[]{:S(2)}, u32[]{:S(2)}) %collective-permute-start.15) | collective-permute-done | bytes 655392 | tf_op jit(solution)/shard_map/ppermute | solution.py:181
  426.8 5.1 fusion.19
  434.1 3.2 copy.91
  437.4 99.0 %all-reduce.18.cloned.1.call-done = (f32[160,768]{1,0:T(8,128)}, f32[128,640]{1,0:T(8,128)}, f32[160,4,256]{2,1,0:T(4,128)}, f32[160,4,256]{2,1,0:T(4,128)}, f32[256,640]{1,0:T(8,128)}) async-done(((f32[160,768]{1,0:T(8,128)}, f32[128,640]{1,0:T(8,128)}, f32[160,4,256]{2,1,0:T(4,128)}, f32[160,4,256]{2,1,0:T(4,128)}, f32[256,640]{1,0:T(8,128)}), (f32[160,768]{1,0:T(8,128)}, f32[128,640]{1,0:T(8,128)}, ...) | async-done | bytes 2785296 | tf_op jit(solution)/shard_map/psum | solution.py:188
  536.4 39.5 %psum.47 = f32[3072]{0:T(1024)S(1)} all-reduce(f32[3072]{0:T(1024)S(1)} %constant_dynamic-update-slice_fusion), channel_id=1, replica_groups=mesh['z'=4,'core'=2,'shard'=4] {'z','core','shard'}, use_global_device_ids=true, to_apply=%region_32.33 | all-reduce | flops 3072 | bytes 24576 | tf_op jit(solution)/shard_map/psum | solution.py:403
  (295 shorter events, 116.6 us)
Async XLA Ops:
  7.2 13.5 %copy-start = (bf16[512,640]{1,0:T(8,128)(2,1)S(1)}, bf16[512,640]{1,0:T(8,128)(2,1)}, u32[]{:S(2)}) copy-start(bf16[512,640]{1,0:T(8,128)(2,1)} %param.25) | copy-start | bytes 1966084
  7.2 6.4 %copy-start.36 = (bf16[160,2048]{1,0:T(8,128)(2,1)S(1)}, bf16[160,2048]{1,0:T(8,128)(2,1)}, u32[]{:S(2)}) copy-start(bf16[160,2048]{1,0:T(8,128)(2,1)} %param.23) | copy-start | bytes 1966084
  7.2 38.6 %all-gather.12.cloned.1.call-start = ((), (), s32[]{:S(2)}) async-start(), calls=%async_computation.3 | async-start | bytes 1474560 | tf_op jit(solution)/shard_map/all_gather | solution.py:221
  11.6 5.6 copy-start.37
  13.5 63.6 %all-gather.6.cloned.1.call-start = ((), (), s32[]{:S(2)}) async-start(), calls=%async_computation | async-start | bytes 1638400 | tf_op jit(solution)/shard_map/all_gather | solution.py:221
  16.1 5.4 copy-start.42
  17.1 91.3 %all-gather.8.cloned.1.call-start = ((), (), s32[]{:S(2)}) async-start(), calls=%async_computation.1 | async-start | bytes 1638400 | tf_op jit(solution)/shard_map/all_gather | solution.py:221
  20.6 118.8 %all-gather.10.cloned.1.call-start = ((), (), s32[]{:S(2)}) async-start(), calls=%async_computation.2 | async-start | bytes 1638400 | tf_op jit(solution)/shard_map/all_gather | solution.py:221
  21.5 514.9 %all-reduce.18.cloned.1.call-start = ((), (), s32[]{:S(2)}) async-start(), calls=%async_computation.4 | async-start | bytes 5570560 | tf_op jit(solution)/shard_map/psum | solution.py:188
  36.0 9.9 %collective-permute-start.1 = (bf16[4,128,640]{2,1,0:T(8,128)(2,1)S(1)}, bf16[4,128,640]{2,1,0:T(8,128)(2,1)S(1)}, u32[]{:S(2)}, u32[]{:S(2)}) collective-permute-start(bf16[4,128,640]{2,1,0:T(8,128)(2,1)S(1)} %all_gather.22), channel_id=1, source_target_pairs={{0,4},{4,0},{1,5},{5,1},{2,6},{6,2},{3,7},{7,3},{8,12},{12,8},{9,1... | collective-permute-start | bytes 1966088 | tf_op jit(solution)/shard_map/ppermute | solution.py:161
  40.1 101.3 %copy-start.14 = (bf16[1024,640]{0,1:T(8,128)(2,1)}, bf16[1024,640]{0,1:T(8,128)(2,1)S(1)}, u32[]{:S(2)}) copy-start(bf16[1024,640]{0,1:T(8,128)(2,1)S(1)} %copy.69) | copy-start | bytes 3932164
  40.6 6.6 %copy-start.43 = (f32[1024]{0:T(1024)}, f32[1024]{0:T(1024)S(1)}, u32[]{:S(2)}) copy-start(f32[1024]{0:T(1024)S(1)} %fusion.25) | copy-start | bytes 12292
  45.9 93.6 %collective-permute-start = (bf16[4,96,1536]{2,1,0:T(8,128)(2,1)}, bf16[4,96,1536]{2,1,0:T(8,128)(2,1)}, u32[]{:S(2)}, u32[]{:S(2)}) collective-permute-start(bf16[4,96,1536]{2,1,0:T(8,128)(2,1)} %bitcast.192), channel_id=1, source_target_pairs={{0,4},{4,0},{1,5},{5,1},{2,6},{6,2},{3,7},{7,3},{8,12},{12,8},{9,1... | collective-permute-start | bytes 3538952 | tf_op jit(solution)/shard_map/ppermute | solution.py:161
  77.1 130.5 %collective-permute-start.2 = (bf16[4,160,1024]{2,1,0:T(8,128)(2,1)}, bf16[4,160,1024]{2,1,0:T(8,128)(2,1)}, u32[]{:S(2)}, u32[]{:S(2)}) collective-permute-start(bf16[4,160,1024]{2,1,0:T(8,128)(2,1)} %all-gather.6.cloned.1.call-done), channel_id=1, source_target_pairs={{0,4},{4,0},{1,5},{5,1},{2,6},{6,2},{3,7},{7,3},{8,12},{12,8},{9,1... | collective-permute-start | bytes 3932168 | tf_op jit(solution)/shard_map/ppermute | solution.py:161
  108.4 102.4 %collective-permute-start.3 = (bf16[4,160,1024]{2,1,0:T(8,128)(2,1)}, bf16[4,160,1024]{2,1,0:T(8,128)(2,1)}, u32[]{:S(2)}, u32[]{:S(2)}) collective-permute-start(bf16[4,160,1024]{2,1,0:T(8,128)(2,1)} %all-gather.8.cloned.1.call-done), channel_id=1, source_target_pairs={{0,4},{4,0},{1,5},{5,1},{2,6},{6,2},{3,7},{7,3},{8,12},{12,8},{9,1... | collective-permute-start | bytes 3932168 | tf_op jit(solution)/shard_map/ppermute | solution.py:161
  139.5 75.4 %collective-permute-start.4 = (bf16[4,256,640]{2,1,0:T(8,128)(2,1)}, bf16[4,256,640]{2,1,0:T(8,128)(2,1)}, u32[]{:S(2)}, u32[]{:S(2)}) collective-permute-start(bf16[4,256,640]{2,1,0:T(8,128)(2,1)} %all-gather.10.cloned.1.call-done), channel_id=1, source_target_pairs={{0,4},{4,0},{1,5},{5,1},{2,6},{6,2},{3,7},{7,3},{8,12},{12,8},{9,1... | collective-permute-start | bytes 3932168 | tf_op jit(solution)/shard_map/ppermute | solution.py:161
  145.0 8.3 %copy-start.3 = (bf16[1024,256]{1,0:T(8,128)(2,1)}, bf16[1024,256]{1,0:T(8,128)(2,1)S(1)}, u32[]{:S(2)}) copy-start(bf16[1024,256]{1,0:T(8,128)(2,1)S(1)} %slice.222.value_ref) | copy-start | bytes 1572868
  175.3 7.5 %copy-start.7 = (f32[1024,640]{0,1:T(8,128)}, f32[1024,640]{0,1:T(8,128)S(1)}, u32[]{:S(2)}) copy-start(f32[1024,640]{0,1:T(8,128)S(1)} %get-tuple-element.132) | copy-start | bytes 7864324
  183.1 5.2 copy-start.32
  200.0 6.0 copy-start.49
  292.7 26.1 %collective-permute-start.13 = (f32[4,160,1024]{2,1,0:T(8,128)}, f32[4,160,1024]{2,1,0:T(8,128)}, u32[]{:S(2)}, u32[]{:S(2)}) collective-permute-start(f32[4,160,1024]{2,1,0:T(8,128)} %bitcast.22), channel_id=1, source_target_pairs={{0,4},{4,0},{1,5},{5,1},{2,6},{6,2},{3,7},{7,3},{8,12},{12,8},{9,1... | collective-permute-start | bytes 7864328 | tf_op jit(solution)/shard_map/ppermute | solution.py:161
  301.2 13.4 %collective-permute-start.5 = (f32[4,160,768]{2,1,0:T(8,128)}, f32[4,160,768]{2,1,0:T(8,128)}, u32[]{:S(2)}, u32[]{:S(2)}) collective-permute-start(f32[4,160,768]{2,1,0:T(8,128)} %bitcast.34), channel_id=1, source_target_pairs={{0,4},{4,0},{1,5},{5,1},{2,6},{6,2},{3,7},{7,3},{8,12},{12,8},{9,1... | collective-permute-start | bytes 5898248 | tf_op jit(solution)/shard_map/ppermute | solution.py:161
  301.2 32.9 %collective-permute-start.17 = (f32[4,160,1024]{2,1,0:T(8,128)}, f32[4,160,1024]{2,1,0:T(8,128)}, u32[]{:S(2)}, u32[]{:S(2)}) collective-permute-start(f32[4,160,1024]{2,1,0:T(8,128)} %bitcast.24), channel_id=1, source_target_pairs={{0,4},{4,0},{1,5},{5,1},{2,6},{6,2},{3,7},{7,3},{8,12},{12,8},{9,1... | collective-permute-start | bytes 7864328 | tf_op jit(solution)/shard_map/ppermute | solution.py:161
  301.7 9.4 %collective-permute-start.9 = (f32[4,128,640]{2,1,0:T(8,128)}, f32[4,128,640]{2,1,0:T(8,128)}, u32[]{:S(2)}, u32[]{:S(2)}) collective-permute-start(f32[4,128,640]{2,1,0:T(8,128)} %fusion.33), channel_id=1, source_target_pairs={{0,4},{4,0},{1,5},{5,1},{2,6},{6,2},{3,7},{7,3},{8,12},{12,8},{9,1... | collective-permute-start | bytes 3932168 | tf_op jit(solution)/shard_map/ppermute | solution.py:161
  301.7 37.0 %collective-permute-start.21 = (f32[4,256,640]{2,1,0:T(8,128)}, f32[4,256,640]{2,1,0:T(8,128)}, u32[]{:S(2)}, u32[]{:S(2)}) collective-permute-start(f32[4,256,640]{2,1,0:T(8,128)} %bitcast.20), channel_id=1, source_target_pairs={{0,4},{4,0},{1,5},{5,1},{2,6},{6,2},{3,7},{7,3},{8,12},{12,8},{9,1... | collective-permute-start | bytes 7864328 | tf_op jit(solution)/shard_map/ppermute | solution.py:161
  313.1 17.7 %collective-permute-start.10 = (f32[2,128,640]{2,1,0:T(8,128)S(1)}, f32[2,128,640]{2,1,0:T(8,128)}, u32[]{:S(2)}, u32[]{:S(2)}) collective-permute-start(f32[2,128,640]{2,1,0:T(8,128)S(1)} %dynamic-slice_bitcast_fusion.7), channel_id=1, source_target_pairs={{0,1},{1,0},{2,3},{3,2},{4,5},{5,4},{6,7},{7,6},{8,9},{9,8},{10,11... | collective-permute-start | bytes 1966088 | tf_op jit(solution)/shard_map/ppermute | solution.py:181
  318.2 33.7 %collective-permute-start.6 = (f32[2,160,768]{2,1,0:T(8,128)}, f32[2,160,768]{2,1,0:T(8,128)}, u32[]{:S(2)}, u32[]{:S(2)}) collective-permute-start(f32[2,160,768]{2,1,0:T(8,128)} %dynamic-slice_bitcast_fusion.3), channel_id=1, source_target_pairs={{0,2},{1,3},{2,0},{3,1},{4,6},{5,7},{6,4},{7,5},{8,10},{9,11},{10,... | collective-permute-start | bytes 2949128 | tf_op jit(solution)/shard_map/ppermute | solution.py:181
  321.1 11.6 %copy-start.19 = (f32[4,160,1024]{2,1,0:T(8,128)}, f32[4,160,1024]{2,1,0:T(8,128)S(1)}, u32[]{:S(2)}) copy-start(f32[4,160,1024]{2,1,0:T(8,128)S(1)} %add.360) | copy-start | bytes 7864324
  321.1 13.0 %copy-start.28 = (f32[640,1024]{1,0:T(8,128)S(1)}, f32[640,1024]{1,0:T(8,128)}, u32[]{:S(2)}) copy-start(f32[640,1024]{1,0:T(8,128)} %fusion.130) | copy-start | bytes 7864324
  322.4 36.5 %collective-permute-start.14 = (f32[2,160,1024]{2,1,0:T(8,128)}, f32[2,160,1024]{2,1,0:T(8,128)}, u32[]{:S(2)}, u32[]{:S(2)}) collective-permute-start(f32[2,160,1024]{2,1,0:T(8,128)} %dynamic-slice_bitcast_fusion.2), channel_id=1, source_target_pairs={{0,1},{1,0},{2,3},{3,2},{4,5},{5,4},{6,7},{7,6},{8,9},{9,8},{10,11... | collective-permute-start | bytes 3932168 | tf_op jit(solution)/shard_map/ppermute | solution.py:181
  332.7 17.5 %collective-permute-start.11 = (f32[128,640]{1,0:T(8,128)}, f32[128,640]{1,0:T(8,128)}, u32[]{:S(2)}, u32[]{:S(2)}) collective-permute-start(f32[128,640]{1,0:T(8,128)} %dynamic-slice_bitcast_fusion.9), channel_id=1, source_target_pairs={{0,2},{1,3},{2,0},{3,1},{4,6},{5,7},{6,4},{7,5},{8,10},{9,11},{10,... | collective-permute-start | bytes 983048 | tf_op jit(solution)/shard_map/ppermute | solution.py:181
  338.1 40.2 %collective-permute-start.18 = (f32[2,160,1024]{2,1,0:T(8,128)S(1)}, f32[2,160,1024]{2,1,0:T(8,128)}, u32[]{:S(2)}, u32[]{:S(2)}) collective-permute-start(f32[2,160,1024]{2,1,0:T(8,128)S(1)} %dynamic-slice_bitcast_fusion.1), channel_id=1, source_target_pairs={{0,2},{1,3},{2,0},{3,1},{4,6},{5,7},{6,4},{7,5},{8,10},{9,11},{10,... | collective-permute-start | bytes 3932168 | tf_op jit(solution)/shard_map/ppermute | solution.py:181
  341.5 10.4 %copy-start.24 = (f32[4,160,768]{2,1,0:T(8,128)S(1)}, f32[4,160,768]{2,1,0:T(8,128)}, u32[]{:S(2)}) copy-start(f32[4,160,768]{2,1,0:T(8,128)} %copy-done.23) | copy-start | bytes 5898244
  341.6 17.3 %copy-start.20 = (f32[4,160,1024]{2,1,0:T(8,128)S(1)}, f32[4,160,1024]{2,1,0:T(8,128)}, u32[]{:S(2)}) copy-start(f32[4,160,1024]{2,1,0:T(8,128)} %copy-done.19) | copy-start | bytes 7864324
  341.6 64.6 %collective-permute-start.22 = (f32[2,256,640]{2,1,0:T(8,128)S(1)}, f32[2,256,640]{2,1,0:T(8,128)S(1)}, u32[]{:S(2)}, u32[]{:S(2)}) collective-permute-start(f32[2,256,640]{2,1,0:T(8,128)S(1)} %dynamic-slice_bitcast_fusion), channel_id=1, source_target_pairs={{0,2},{1,3},{2,0},{3,1},{4,6},{5,7},{6,4},{7,5},{8,10},{9,11},{10,... | collective-permute-start | bytes 3932168 | tf_op jit(solution)/shard_map/ppermute | solution.py:181
  353.3 25.0 %copy-start.22 = (f32[4,160,1024]{2,1,0:T(8,128)S(1)}, f32[4,160,1024]{2,1,0:T(8,128)}, u32[]{:S(2)}) copy-start(f32[4,160,1024]{2,1,0:T(8,128)} %copy-done.21) | copy-start | bytes 7864324
  353.3 55.6 %collective-permute-start.7 = (f32[160,768]{1,0:T(8,128)S(1)}, f32[160,768]{1,0:T(8,128)S(1)}, u32[]{:S(2)}, u32[]{:S(2)}) collective-permute-start(f32[160,768]{1,0:T(8,128)S(1)} %dynamic-slice_bitcast_fusion.8), channel_id=1, source_target_pairs={{0,1},{1,0},{2,3},{3,2},{4,5},{5,4},{6,7},{7,6},{8,9},{9,8},{10,11... | collective-permute-start | bytes 1474568 | tf_op jit(solution)/shard_map/ppermute | solution.py:181
  360.5 58.7 %collective-permute-start.15 = (f32[160,1024]{1,0:T(8,128)S(1)}, f32[160,1024]{1,0:T(8,128)S(1)}, u32[]{:S(2)}, u32[]{:S(2)}) collective-permute-start(f32[160,1024]{1,0:T(8,128)S(1)} %dynamic-slice_bitcast_fusion.6), channel_id=1, source_target_pairs={{0,2},{1,3},{2,0},{3,1},{4,6},{5,7},{6,4},{7,5},{8,10},{9,11},{10,... | collective-permute-start | bytes 1966088 | tf_op jit(solution)/shard_map/ppermute | solution.py:181
  380.7 39.7 %collective-permute-start.19 = (f32[160,1024]{1,0:T(8,128)}, f32[160,1024]{1,0:T(8,128)}, u32[]{:S(2)}, u32[]{:S(2)}) collective-permute-start(f32[160,1024]{1,0:T(8,128)} %dynamic-slice_bitcast_fusion.5), channel_id=1, source_target_pairs={{0,1},{1,0},{2,3},{3,2},{4,5},{5,4},{6,7},{7,6},{8,9},{9,8},{10,11... | collective-permute-start | bytes 1966088 | tf_op jit(solution)/shard_map/ppermute | solution.py:181
  408.3 14.8 %collective-permute-start.23 = (f32[256,640]{1,0:T(8,128)}, f32[256,640]{1,0:T(8,128)}, u32[]{:S(2)}, u32[]{:S(2)}) collective-permute-start(f32[256,640]{1,0:T(8,128)} %dynamic-slice_bitcast_fusion.4), channel_id=1, source_target_pairs={{0,1},{1,0},{2,3},{3,2},{4,5},{5,4},{6,7},{7,6},{8,9},{9,8},{10,11... | collective-permute-start | bytes 1966088 | tf_op jit(solution)/shard_map/ppermute | solution.py:181
  426.8 5.1 copy-start.44
  426.8 5.2 copy-start.11
  536.4 43.7 %copy-start.41 = (f32[160,768]{1,0:T(8,128)S(1)}, f32[160,768]{1,0:T(8,128)}, u32[]{:S(2)}) copy-start(f32[160,768]{1,0:T(8,128)} %get-tuple-element.125) | copy-start | bytes 1474564
  536.4 41.7 %collective-permute-start.12 = (f32[128,640]{1,0:T(8,128)}, f32[128,640]{1,0:T(8,128)S(1)}, u32[]{:S(2)}, u32[]{:S(2)}) collective-permute-start(f32[128,640]{1,0:T(8,128)} %get-tuple-element.126), channel_id=1, source_target_pairs={{0,4},{4,0},{1,5},{5,1},{2,6},{6,2},{3,7},{7,3},{8,12},{12,8},{9,1... | collective-permute-start | bytes 983048 | tf_op jit(solution)/shard_map/ppermute | solution.py:161
  576.5 3.5 collective-permute-start.8
  577.1 6.5 %collective-permute-start.16 = (f32[160,4,256]{2,1,0:T(4,128)}, f32[160,4,256]{2,1,0:T(4,128)S(1)}, u32[]{:S(2)}, u32[]{:S(2)}) collective-permute-start(f32[160,4,256]{2,1,0:T(4,128)} %get-tuple-element.127), channel_id=1, source_target_pairs={{0,4},{4,0},{1,5},{5,1},{2,6},{6,2},{3,7},{7,3},{8,12},{12,8},{9,1... | collective-permute-start | bytes 1966088 | tf_op jit(solution)/shard_map/ppermute | solution.py:161
  577.6 9.6 %collective-permute-start.20 = (f32[160,4,256]{2,1,0:T(4,128)}, f32[160,4,256]{2,1,0:T(4,128)S(1)}, u32[]{:S(2)}, u32[]{:S(2)}) collective-permute-start(f32[160,4,256]{2,1,0:T(4,128)} %get-tuple-element.128), channel_id=1, source_target_pairs={{0,4},{4,0},{1,5},{5,1},{2,6},{6,2},{3,7},{7,3},{8,12},{12,8},{9,1... | collective-permute-start | bytes 1966088 | tf_op jit(solution)/shard_map/ppermute | solution.py:161
  577.6 14.3 %collective-permute-start.24 = (f32[256,640]{1,0:T(8,128)}, f32[256,640]{1,0:T(8,128)S(1)}, u32[]{:S(2)}, u32[]{:S(2)}) collective-permute-start(f32[256,640]{1,0:T(8,128)} %get-tuple-element.129), channel_id=1, source_target_pairs={{0,4},{4,0},{1,5},{5,1},{2,6},{6,2},{3,7},{7,3},{8,12},{12,8},{9,1... | collective-permute-start | bytes 1966088 | tf_op jit(solution)/shard_map/ppermute | solution.py:161
  (35 other events, 89.0 us)
Sparse Core Ops, SparseCore 0:
  13.6 32.1 all-gather.11
  48.3 28.7 all-gather.5
  79.5 28.7 all-gather.7
  110.6 28.7 all-gather.9
  425.5 110.8 all-reduce.17
